TPU v7x, 512 devices: a whole 4x8x8 slice. The times are simulated.
512 devices in a mesh: dp: 64 (over y, x, z_hi), fsdp: 8 (over z_lo, core).
Axes of the slice: x: 4, y: 8, z: 8 (z_hi: 2, z_lo: 4; z = z_hi * 4 + z_lo), core: 2. Of those that a mesh axis runs over, the one named last changes fastest.
Arguments:
- tokens: bfloat16 [24576, 4096], P('dp'), may hold values from -6 to 6
- grad_out: bfloat16 [24576, 11008], P('dp', 'fsdp'), may hold values from -0.375 to 0.375
- subspace_basis: bfloat16 [4096, 512], P('dp'), may hold values from -0.09375 to 0.09375
- first_moment: float32 [512, 11008], P('dp', 'fsdp'), may hold values from -18 to 18
- second_moment: float32 [512, 11008], P('dp', 'fsdp'), may hold values from 0.03 to 0.3
Outputs:
- new_first: float32 [512, 11008], P('dp', 'fsdp')
- new_second: float32 [512, 11008], P('dp', 'fsdp')
- weight_update: bfloat16 [4096, 11008], P('dp')
All inputs are finite; a program needn't handle non-finite values.
Results may differ from a plain program's by a relative error of at most 0.0052.
Values may be sent and summed in bfloat16 or wider, within the bound.
A program may use at most 64 MiB of HBM per device.

v0:
```python
import jax
import jax.numpy as jnp
from jax import lax
from jax.sharding import PartitionSpec as P

beta_one = 0.9
beta_two = 0.999
correct_one = 1.0 - 0.9**10
correct_two = 1.0 - 0.999**10


def on_device(tokens, grad_out, subspace_basis, first_moment, second_moment):
    projected = jnp.dot(
        tokens,
        lax.all_gather(subspace_basis, "dp", axis=0, tiled=True),
        preferred_element_type=jnp.float32,
    ).astype(jnp.bfloat16)
    low_grad = lax.psum_scatter(
        lax.dot_general(
            projected, grad_out, (((0,), (0,)), ((), ())), preferred_element_type=jnp.float32
        ),
        "dp",
        scatter_dimension=0,
        tiled=True,
    )
    new_first = beta_one * first_moment + (1.0 - beta_one) * low_grad
    new_second = beta_two * second_moment + (1.0 - beta_two) * low_grad * low_grad
    direction = (new_first / correct_one / (jnp.sqrt(new_second / correct_two) + 1e-08)).astype(
        jnp.bfloat16
    )
    update_block = jnp.dot(
        subspace_basis,
        lax.all_gather(direction, "dp", axis=0, tiled=True),
        preferred_element_type=jnp.float32,
    ).astype(jnp.bfloat16)
    weight_update = lax.all_gather(update_block, "fsdp", axis=1, tiled=True)
    return (new_first, new_second, weight_update)


def solution(mesh):
    placed = (P("dp", None), P("dp", "fsdp"), P("dp", None), P("dp", "fsdp"), P("dp", "fsdp"))
    return jax.shard_map(
        on_device,
        mesh=mesh,
        in_specs=placed,
        out_specs=(P("dp", "fsdp"), P("dp", "fsdp"), P("dp", None)),
        check_vma=False,
    )
```

profile of v0, /device:TPU:1, one launch (start us, length us, event | category | flops | bytes accessed | tf_op | source)
XLA Modules:
  0.0 1211.4 jit_solution(14226909767976945609)
XLA Ops:
  7.2 0.0 copy-start
  7.2 0.0 all-gather.5.cloned.1.call-start
  7.2 0.7 all-gather.5.cloned.1.call-update
  7.9 0.0 all-reduce.3.cloned.1.call-start
  8.0 165.2 %all-gather.5.cloned.1.call-done = bf16[4096,512]{1,0:T(8,128)(2,1)} async-done(((bf16[64,512]{1,0:T(8,128)(2,1)}), bf16[4096,512]{1,0:T(8,128)(2,1)}) %all-gather.5.cloned.1.call-update) | async-done | bytes 4194320 | tf_op jit(solution)/shard_map/all_gather | solution.py:15
  173.2 0.0 copy-done
  173.2 6.8 fusion.1
  180.0 0.0 copy-start.2
  180.0 0.0 copy-start.3
  180.0 0.0 copy-start.1
  180.0 0.0 all-reduce.3.cloned.1.call-update
  180.0 0.0 all-gather.7.cloned.1.call-start
  180.0 1.3 dynamic-slice
  182.0 804.3 %all-reduce.3.cloned.1.call-done = f32[512,1376]{1,0:T(8,128)} async-done(((f32[512,1376]{1,0:T(8,128)}), f32[512,1376]{1,0:T(8,128)}) %all-reduce.3.cloned.1.call-update) | async-done | bytes 2818064
  986.3 0.0 copy-done.2
  986.3 0.0 copy-done.3
  986.3 1.4 divide_convert_fusion
  987.7 0.0 all-gather.7.cloned.1.call-update
  987.7 0.0 all-gather.9.cloned.1.call-start
  987.8 171.6 %all-gather.7.cloned.1.call-done = bf16[512,1376]{1,0:T(8,128)(2,1)} async-done(((bf16[8,1376]{1,0:T(8,128)(2,1)}), bf16[512,1376]{1,0:T(8,128)(2,1)}) %all-gather.7.cloned.1.call-update) | async-done | bytes 1409040 | tf_op jit(solution)/shard_map/all_gather | solution.py:33
  1159.4 0.0 copy-done.1
  1159.4 2.4 fusion
  1161.8 0.0 all-gather.9.cloned.1.call-update
  1161.8 36.0 %all-gather.9.cloned.1.call-done = bf16[8,1376,64]{1,2,0:T(8,128)(2,1)} async-done(((bf16[1,1376,64]{1,2,0:T(8,128)(2,1)}), bf16[8,1376,64]{1,2,0:T(8,128)(2,1)}) %all-gather.9.cloned.1.call-update) | async-done | bytes 1409040 | tf_op jit(solution)/shard_map/all_gather | solution.py:36
  1197.8 3.3 copy.9
  1201.0 3.8 reshape.7
Async XLA Ops:
  7.2 166.0 %copy-start = (bf16[384,4096]{1,0:T(8,128)(2,1)S(1)}, bf16[384,4096]{1,0:T(8,128)(2,1)}, u32[]{:S(2)}) copy-start(bf16[384,4096]{1,0:T(8,128)(2,1)} %param.5) | copy-start | bytes 9437188
  7.2 166.0 %all-gather.5.cloned.1.call-start = ((), (), s32[]{:S(2)}) async-start(), calls=%async_computation | async-start | bytes 4259840 | tf_op jit(solution)/shard_map/all_gather | solution.py:15
  7.9 978.3 %all-reduce.3.cloned.1.call-start = ((), (), s32[]{:S(2)}) async-start(), calls=%async_computation.3 | async-start | bytes 5767168
  180.0 806.3 %copy-start.2 = (f32[8,1376]{1,0:T(8,128)S(1)}, f32[8,1376]{1,0:T(8,128)}, u32[]{:S(2)}) copy-start(f32[8,1376]{1,0:T(8,128)} %param.9) | copy-start | bytes 132100
  180.0 806.3 %copy-start.3 = (f32[8,1376]{1,0:T(8,128)S(1)}, f32[8,1376]{1,0:T(8,128)}, u32[]{:S(2)}) copy-start(f32[8,1376]{1,0:T(8,128)} %param.8) | copy-start | bytes 132100
  180.0 979.4 %copy-start.1 = (bf16[64,512]{1,0:T(8,128)(2,1)S(1)}, bf16[64,512]{1,0:T(8,128)(2,1)}, u32[]{:S(2)}) copy-start(bf16[64,512]{1,0:T(8,128)(2,1)} %param.7) | copy-start | bytes 196612
  180.0 979.4 %all-gather.7.cloned.1.call-start = ((), (), s32[]{:S(2)}) async-start(), calls=%async_computation.1 | async-start | bytes 1464320 | tf_op jit(solution)/shard_map/all_gather | solution.py:33
  987.7 210.0 %all-gather.9.cloned.1.call-start = ((), (), s32[]{:S(2)}) async-start(), calls=%async_computation.2 | async-start | bytes 1622016 | tf_op jit(solution)/shard_map/all_gather | solution.py:36
Sparse Core Ops, SparseCore 0:
  12.5 160.5 all-gather.4
  180.1 806.1 all-reduce.2
  992.1 167.1 all-gather.6
  1162.1 35.6 all-gather.8
where the time goes:
time: 1210 us
  waiting for transfers between devices  1180 us (98%)
  between operations  14.4 us (1%)
    unnamed x5, waiting for transfers between devices  805 us
    all_gather x1, waiting for transfers between devices, on_device(): lax.all_gather(direction, 'dp', axis=0, tiled=True)  172 us
    all_gather x1, waiting for transfers between devices, on_device(): lax.all_gather(subspace_basis, 'dp', axis=0, tiled=True)  165 us
    all_gather x1, waiting for transfers between devices, on_device(): weight_update = lax.all_gather(update_block, 'fsdp', axis=1, tiled=True)  36 us
  transfers between devices with their start and end apart: 4, of which 4 were waited for; matrix products, arithmetic and copies ran while one was open for 0% of the time, Pallas kernels for 0%

commit v1 on v0

v1 whole, which is shorter than its diff:
```python
import functools

import jax
import jax.numpy as jnp
from jax import lax
from jax.experimental import pallas as pl
from jax.experimental.pallas import tpu as pltpu
from jax.sharding import PartitionSpec as P

beta_one = 0.9
beta_two = 0.999
correct_one = 1.0 - 0.9**10
correct_two = 1.0 - 0.999**10

X = 4
Z_HI, Z_LO, CORES = 2, 4, 2
RING = Z_HI * Z_LO
PART_A = 640
COPIES = 160

MESH = pl.DeviceIdType.MESH
F32, BF16 = jnp.float32, jnp.bfloat16


def wrap(value, n):
    return lax.rem(value + n, n)


def interleave(*steps):
    steps = list(steps)
    while steps:
        steps = [step for step in steps if next(step, "end") != "end"]


def kernel(
    Y, tokens, grad, basis, first, second,
    new_first, new_second, update,
    tok_v, grad_v, basis_v, bas, proj, first_v, second_v, nf_v, ns_v,
    own_a, own_b, mid_a, mid_b, sum_a, sum_b,
    sa1, ra1, sa2, ra2, sb1, rb1, sb2, rb2, pair_sa, pair_ra, pair_sb, pair_rb,
    dir_a, dir_b, send_a, send_b, upd_a, upd_b,
    send_sem, recv_sem, load_sem,
):
    dp, fs = lax.axis_index("dp"), lax.axis_index("fsdp")
    zh, xy = lax.rem(dp, Z_HI), dp // Z_HI
    x, y = lax.rem(xy, X), xy // X
    core, zl = lax.rem(fs, CORES), fs // CORES
    z = zh * Z_LO + zl
    half_tokens = tok_v.shape[0]
    depth = bas.shape[4]
    rows = basis_v.shape[1]
    cols = grad.shape[1]
    parts = ((0, PART_A), (PART_A, cols - PART_A))

    def device(y_, x_, z_, core_):
        return ((y_ * X + x_) * Z_HI + z_ // Z_LO, lax.rem(z_, Z_LO) * CORES + core_)

    at_y = lambda t: device(t, x, z, core)
    at_x = lambda t: device(y, t, z, core)
    at_z = lambda t: device(y, x, t, core)
    sibling = device(y, x, z, 1 - core)
    partner = at_z(wrap(z + Z_LO, RING))

    sent = []

    def send(src, dst, target):
        k = len(sent)
        copy = pltpu.make_async_remote_copy(
            src_ref=src, dst_ref=dst, send_sem=send_sem.at[k], recv_sem=recv_sem.at[k],
            device_id=target, device_id_type=MESH,
        )
        copy.start()
        sent.append(copy)
        return copy

    def ring_gather(n, pos, target, block, half=None, arrived=None):
        flying = {}
        for s in range(n // 2):
            for d, h in ((1, 0), (-1, 1)):
                t = wrap(pos - d * s, n)
                if s:
                    flying[d].wait_recv()
                    if arrived:
                        arrived(t)
                if s < n // 2 - 1:
                    ref = block(t)
                elif half:
                    ref = half(t, h)
                elif d == 1:
                    ref = block(t)
                else:
                    flying.pop(d, None)
                    continue
                flying[d] = send(ref, ref, target(wrap(pos + d, n)))
            yield
        for copy in flying.values():
            copy.wait_recv()
        if arrived:
            arrived(wrap(pos + n // 2, n))

    def ring_scatter(n, pos, target, own, sbuf, rbuf, result, split):
        flying, last = {}, {}
        size = own.shape[1]
        for s in range(n // 2):
            for i, d in ((0, 1), (1, -1)):
                t = wrap(pos + d * (n // 2 - s), n)
                whole = pl.ds(0, size)
                part = pl.ds(i * (size // 2), size // 2) if split else whole
                if s == 0:
                    if not split and i == 1:
                        continue
                    sbuf[i, 0, part] = own[t, part].astype(BF16)
                    flying[i] = send(sbuf.at[i, 0, part], rbuf.at[i, 0, part], target(wrap(pos + d, n)))
                    last[i] = (0, part)
                    continue
                if i in flying:
                    flying[i].wait_recv()
                    before, taken = last[i]
                    sbuf[i, s, taken] = (own[t, taken] + rbuf[i, before, taken].astype(F32)).astype(BF16)
                    if split and s == 1:
                        other = pl.ds((1 - i) * (size // 2), size // 2)
                        sbuf[i, s, other] = own[t, other].astype(BF16)
                else:
                    sbuf[i, s] = own[t].astype(BF16)
                flying[i] = send(sbuf.at[i, s], rbuf.at[i, s], target(wrap(pos + d, n)))
                last[i] = (s, whole)
            yield
        total = own[pos]
        for i in flying:
            flying[i].wait_recv()
        if n == 2 and split:
            low = rbuf[0, 0, pl.ds(0, size // 2)].astype(F32)
            high = rbuf[1, 0, pl.ds(size // 2, size // 2)].astype(F32)
            total = total + jnp.concatenate([low, high], axis=0)
        else:
            for i in flying:
                total = total + rbuf[i, last[i][0]].astype(F32)
        result[...] = total.reshape(result.shape)

    loads = [
        pltpu.make_async_copy(basis, basis_v.at[zh], load_sem.at[0]),
        pltpu.make_async_copy(tokens.at[pl.ds(core * half_tokens, half_tokens)], tok_v, load_sem.at[1]),
        pltpu.make_async_copy(grad, grad_v, load_sem.at[2]),
        pltpu.make_async_copy(first, first_v.at[zh], load_sem.at[3]),
        pltpu.make_async_copy(second, second_v.at[zh], load_sem.at[4]),
    ]
    for load in loads:
        load.start()

    barrier = pltpu.get_barrier_semaphore()
    near = [at_z(wrap(z + k - RING, RING)) for k in range(1, RING)] + [sibling]
    for d in (1, -1):
        near += [at_y(wrap(y + d, Y)), at_x(wrap(x + d, X))]
    for target in near:
        pl.semaphore_signal(barrier, inc=1, device_id=target, device_id_type=MESH)
    pl.semaphore_wait(barrier, len(near))

    loads[0].wait()
    share = pl.ds(core * (rows // 2), rows // 2)
    lanes = pl.ds(zl * depth_of(bas), depth_of(bas))
    bas[y, x, zh, share] = basis_v[zh, share, lanes]
    pair = send(bas.at[y, x, zh, share], bas.at[y, x, zh, share], partner)
    loads[3].wait()
    loads[4].wait()
    basis_pair = send(basis_v.at[zh], basis_v.at[zh], partner)
    first_pair = send(first_v.at[zh], first_v.at[zh], partner)
    second_pair = send(second_v.at[zh], second_v.at[zh], partner)
    pair.wait_recv()
    interleave(
        ring_gather(
            X, x, at_x,
            lambda t: bas.at[y, t, :, share],
            lambda t, h: bas.at[y, t, pl.ds(h, 1), share],
        )
    )
    to_sibling = []

    def hand_over(t):
        ref = bas.at[t, :, :, share]
        to_sibling.append(send(ref, ref, sibling))

    hand_over(y)
    interleave(
        ring_gather(
            Y, y, at_y,
            lambda t: bas.at[t, :, :, share],
            lambda t, h: bas.at[t, pl.ds(h * (X // 2), X // 2), :, share],
            hand_over,
        )
    )
    for copy in to_sibling:
        copy.wait_recv()

    loads[1].wait()
    mine = pl.ds(core * half_tokens, half_tokens)
    proj[zl, mine] = jnp.dot(
        tok_v[...], bas[...].reshape(-1, depth_of(bas)), preferred_element_type=F32
    ).astype(BF16)
    ref = proj.at[zl, mine]
    beside = [send(ref, ref, sibling)]
    along = [send(ref, ref, at_z(zh * Z_LO + wrap(zl + k - Z_LO, Z_LO))) for k in range(1, Z_LO)]
    loads[2].wait()
    wide = own_a.shape[1] // 16 * 16
    per = depth_of(bas) // wide
    for k in range(Z_LO):
        r = wrap(zl - k, Z_LO)
        if k:
            along[k - 1].wait_recv()
            ref = proj.at[r, mine]
            beside.append(send(ref, ref, sibling))
        beside[k].wait_recv()
        part = lax.dot_general(
            proj[r], grad_v[...], (((0,), (0,)), ((), ())), preferred_element_type=F32
        )
        own_a[pl.ds(r * per, per)] = part[:, :PART_A].reshape(per, wide, PART_A)
        part_b = part[:, PART_A:].reshape(per, X, 16, cols - PART_A)
        for t in range(X):
            own_b[t, pl.ds(r * per, per)] = part_b[:, t]

    basis_pair.wait_recv()
    first_pair.wait_recv()
    second_pair.wait_recv()

    def column_part(number):
        low, width = parts[number]
        total, pair_s, pair_r = ((sum_a, pair_sa, pair_ra), (sum_b, pair_sb, pair_rb))[number]
        if number == 0:
            yield from ring_scatter(Y, y, at_y, own_a, sa1, ra1, mid_a, True)
            yield from ring_scatter(X, x, at_x, mid_a, sa2, ra2, total, False)
        else:
            yield from ring_scatter(X, x, at_x, own_b, sb1, rb1, mid_b, True)
            yield from ring_scatter(Y, y, at_y, mid_b, sb2, rb2, total, False)
        pair_s[...] = total[...].astype(BF16)
        copy = send(pair_s, pair_r, partner)
        yield
        copy.wait_recv()
        low_grad = total[...] + pair_r[...].astype(F32)
        span = pl.ds(low, width)
        old_first = first_v[:, :, span].reshape(low_grad.shape)
        old_second = second_v[:, :, span].reshape(low_grad.shape)
        fresh_first = beta_one * old_first + (1.0 - beta_one) * low_grad
        fresh_second = beta_two * old_second + (1.0 - beta_two) * low_grad * low_grad
        nf_v[:, :, span] = fresh_first.reshape(Z_HI, -1, width)
        ns_v[:, :, span] = fresh_second.reshape(Z_HI, -1, width)
        direction = (
            fresh_first / correct_one / (jnp.sqrt(fresh_second / correct_two) + 1e-08)
        ).astype(BF16)
        whole = (dir_a, dir_b)[number]
        whole[y, x] = direction
        if number == 0:
            yield from ring_gather(X, x, at_x, lambda t: whole.at[y, t])
            yield from ring_gather(
                Y, y, at_y, lambda t: whole.at[t],
                lambda t, h: whole.at[t, pl.ds(h * (X // 2), X // 2)],
            )
        else:
            yield from ring_gather(Y, y, at_y, lambda t: whole.at[t, x])
            yield from ring_gather(
                X, x, at_x, lambda t: whole.at[:, t],
                lambda t, h: whole.at[pl.ds(h * (Y // 2), Y // 2), t],
            )
        out_s, out_r = ((send_a, upd_a), (send_b, upd_b))[number]
        block = jnp.dot(
            basis_v[...].reshape(Z_HI * rows, -1), whole[...].reshape(-1, width),
            preferred_element_type=F32,
        ).astype(BF16)
        out_s[...] = block.reshape(out_s.shape)
        moving = {}
        for step in (1, -1):
            to = wrap(z + step, RING)
            moving[step] = send(out_s.at[to // Z_LO], out_r.at[zl, core], at_z(to))
        for step in (2, -2):
            to = wrap(z + step, RING)
            cut = pl.ds(0 if step > 0 else rows // 2, rows // 2)
            moving[step] = send(out_s.at[to // Z_LO, cut], out_r.at[zl, core, cut], at_z(to))
        out_r[zl, core] = out_s[zh]
        across = [send(out_r.at[zl, core], out_r.at[zl, core], sibling)]
        yield
        for step in (1, -1):
            moving[step].wait_recv()
            ref = out_r.at[wrap(zl - step, Z_LO), core]
            across.append(send(ref, ref, sibling))
        yield
        moving[2].wait_recv()
        moving[-2].wait_recv()
        ref = out_r.at[wrap(zl + 2, Z_LO), core]
        across.append(send(ref, ref, sibling))
        yield
        for copy in across:
            copy.wait_recv()
        for block in range(Z_LO):
            for c in range(CORES):
                at = (block * CORES + c) * cols + low
                update[:, at : at + width] = out_r[block, c]

    interleave(column_part(0), column_part(1))

    stores = [
        pltpu.make_async_copy(nf_v.at[zh], new_first, load_sem.at[5]),
        pltpu.make_async_copy(ns_v.at[zh], new_second, load_sem.at[6]),
    ]
    for store in stores:
        store.start()
    for copy in sent:
        copy.wait_send()
    for store in stores:
        store.wait()


def depth_of(bas):
    return bas.shape[4]


def on_device(Y, tokens, grad, basis, first, second):
    held, width = tokens.shape
    cols = grad.shape[1]
    rows, rank = basis.shape
    own = first.shape[0]
    part_b = cols - PART_A
    deep = rank // Z_LO
    y_rows, pair_rows = rank // Y, Z_HI * own
    assert y_rows == X * pair_rows
    scratch = [
        ((held // 2, width), BF16),
        ((held, cols), BF16),
        ((Z_HI, rows, rank), BF16),
        ((Y, X, Z_HI, rows, deep), BF16),
        ((Z_LO, held, deep), BF16),
        ((Z_HI, own, cols), F32),
        ((Z_HI, own, cols), F32),
        ((Z_HI, own, cols), F32),
        ((Z_HI, own, cols), F32),
        ((Y, y_rows, PART_A), F32),
        ((X, Y, pair_rows, part_b), F32),
        ((X, pair_rows, PART_A), F32),
        ((Y, pair_rows, part_b), F32),
        ((pair_rows, PART_A), F32),
        ((pair_rows, part_b), F32),
    ]
    scratch += [((2, Y // 2, y_rows, PART_A), BF16)] * 2
    scratch += [((2, X // 2, pair_rows, PART_A), BF16)] * 2
    scratch += [((2, X // 2, Y, pair_rows, part_b), BF16)] * 2
    scratch += [((2, Y // 2, pair_rows, part_b), BF16)] * 2
    scratch += [((pair_rows, PART_A), BF16)] * 2
    scratch += [((pair_rows, part_b), BF16)] * 2
    scratch += [
        ((Y, X, pair_rows, PART_A), BF16),
        ((Y, X, pair_rows, part_b), BF16),
        ((Z_HI, rows, PART_A), BF16),
        ((Z_HI, rows, part_b), BF16),
        ((Z_LO, CORES, rows, PART_A), BF16),
        ((Z_LO, CORES, rows, part_b), BF16),
    ]
    anywhere = pl.BlockSpec(memory_space=pl.ANY)
    return pl.pallas_call(
        functools.partial(kernel, Y),
        out_shape=(
            jax.ShapeDtypeStruct(first.shape, F32),
            jax.ShapeDtypeStruct(second.shape, F32),
            jax.ShapeDtypeStruct((rows, Z_LO * CORES * cols), BF16),
        ),
        in_specs=[anywhere] * 5,
        out_specs=(anywhere, anywhere, pl.BlockSpec(memory_space=pltpu.VMEM)),
        scratch_shapes=[pltpu.VMEM(shape, dtype) for shape, dtype in scratch]
        + [
            pltpu.SemaphoreType.DMA((COPIES,)),
            pltpu.SemaphoreType.DMA((COPIES,)),
            pltpu.SemaphoreType.DMA((7,)),
        ],
        compiler_params=pltpu.CompilerParams(
            collective_id=0, has_side_effects=True, vmem_limit_bytes=44 * 2**20
        ),
        cost_estimate=pl.CostEstimate(flops=2 * 10**9, bytes_accessed=10**7, transcendentals=0),
    )(tokens, grad, basis, first, second)


def solution(mesh):
    placed = (P("dp", None), P("dp", "fsdp"), P("dp", None), P("dp", "fsdp"), P("dp", "fsdp"))
    Y = mesh.shape["dp"] // (X * Z_HI)
    return jax.shard_map(
        functools.partial(on_device, Y),
        mesh=mesh,
        in_specs=placed,
        out_specs=(P("dp", "fsdp"), P("dp", "fsdp"), P("dp", None)),
        check_vma=False,
    )
```

time: 1210 us -> 118 us (0.10)
  waiting for transfers between devices: 1180 us -> 0 us
  Pallas kernels: 0 us -> 112 us
  between operations: 14.4 us -> 0.7 us
    unnamed x5 -> x0, waiting for transfers between devices: 805 us -> none
    all_gather x3 -> x0, waiting for transfers between devices: 373 us -> none  [the longest x1 172 us: on_device(): lax.all_gather(direction, 'dp', axis=0, tiled=True)]
    pallas_call x0 -> x1, Pallas kernels: none -> 112 us  [on_device(): pl.pallas_call(functools.partial(kernel, Y), out_shape=(jax.ShapeDtypeStr...]
  transfers between devices with their start and end apart: 4 -> 0, of which waited for: 4 -> 0; matrix products, arithmetic and copies ran while one was open for 0% -> 0% of each run, Pallas kernels for 0% -> 0%
where the time goes in v1:
time: 118 us
  Pallas kernels  112 us (95%)
  local copies, waits for them, and re-layouts  5.97 us (5%)
    pallas_call x1, Pallas kernels, on_device(): pl.pallas_call(functools.partial(kernel, Y), out_shape=(jax.ShapeDtypeStr...  112 us
    unnamed x12, local copies, waits for them, and re-layouts  5.97 us

profile of v1, /device:TPU:1, one launch (start us, length us, event | category | flops | bytes accessed | tf_op | source)
XLA Modules:
  0.0 118.3 jit_solution(3878295929820111601)
XLA Ops:
  0.6 0.0 copy-start.3
  0.6 0.0 copy-start.2
  0.7 0.0 copy-start.1
  0.7 1.7 %copy.8.grad = bf16[384,1376]{1,0:T(8,128)(2,1)S(1)} copy(bf16[384,1376]{0,1:T(8,128)(2,1)} %param.6) | data formatting | bytes 2113536 | tf_op args[1]
  2.4 0.0 copy-done.3
  2.4 0.0 copy-done.2
  2.4 0.0 copy-done.1
  2.4 0.0 copy-start
  2.5 1.9 %copy-done = bf16[384,4096]{1,0:T(8,128)(2,1)S(1)} copy-done((bf16[384,4096]{1,0:T(8,128)(2,1)S(1)}, bf16[384,4096]{1,0:T(8,128)(2,1)}, u32[]{:S(2)}) %copy-start) | copy-done | bytes 3145752
  4.3 111.6 %shard_map.76 = (f32[8,1376]{1,0:T(8,128)S(1)}, f32[8,1376]{1,0:T(8,128)S(1)}, bf16[64,11008]{1,0:T(8,128)(2,1)S(1)}) custom-call(bf16[384,4096]{1,0:T(8,128)(2,1)S(1)} %copy-done, bf16[384,1376]{1,0:T(8,128)(2,1)S(1)} %copy.8.grad, bf16[64,512]{1,0:T(8,128)(2,1)S(1)} %copy-done.1, f32[8,1376]{1,0:T(8,128)S(1)} %copy-done.2, f32[8,1376]{1,0:T(8,128)S(1)} %copy-done.3), custom_call_target="tpu_custom_call" | custom-call | flops 2000000000 | bytes 10000000 | tf_op jit(solution)/shard_map/pallas_call | solution.py:355
  115.9 0.6 copy.12
  116.6 0.6 copy.13
  117.2 1.1 copy.14
Async XLA Ops:
  0.6 1.8 %copy-start.3 = (f32[8,1376]{1,0:T(8,128)S(1)}, f32[8,1376]{1,0:T(8,128)}, u32[]{:S(2)}) copy-start(f32[8,1376]{1,0:T(8,128)} %second.1) | copy-start | bytes 132100
  0.6 1.8 %copy-start.2 = (f32[8,1376]{1,0:T(8,128)S(1)}, f32[8,1376]{1,0:T(8,128)}, u32[]{:S(2)}) copy-start(f32[8,1376]{1,0:T(8,128)} %first.1) | copy-start | bytes 132100
  0.7 1.8 %copy-start.1 = (bf16[64,512]{1,0:T(8,128)(2,1)S(1)}, bf16[64,512]{1,0:T(8,128)(2,1)}, u32[]{:S(2)}) copy-start(bf16[64,512]{1,0:T(8,128)(2,1)} %basis.1) | copy-start | bytes 196612
  2.4 1.9 %copy-start = (bf16[384,4096]{1,0:T(8,128)(2,1)S(1)}, bf16[384,4096]{1,0:T(8,128)(2,1)}, u32[]{:S(2)}) copy-start(bf16[384,4096]{1,0:T(8,128)(2,1)} %tokens.1) | copy-start | bytes 9437188

commit v2 on v0

v2 whole, which is shorter than its diff:
```python
import functools

import jax
import jax.numpy as jnp
from jax import lax
from jax.experimental import pallas as pl
from jax.experimental.pallas import tpu as pltpu
from jax.sharding import PartitionSpec as P

beta_one = 0.9
beta_two = 0.999
correct_one = 1.0 - 0.9**10
correct_two = 1.0 - 0.999**10

X = 4
Z_HI, Z_LO, CORES = 2, 4, 2
RING = Z_HI * Z_LO
PARTS = ((0, 384), (384, 384), (768, 384), (1152, 224))
LAG = 1
COPIES = 200

MESH = pl.DeviceIdType.MESH
F32, BF16 = jnp.float32, jnp.bfloat16


def wrap(value, n):
    return lax.rem(value + n, n)


def interleave(*steps):
    steps = list(steps)
    while steps:
        steps = [step for step in steps if next(step, "end") != "end"]


def kernel(
    Y, tokens, grad, basis, first, second,
    new_first, new_second, update,
    tok_v, grad_v, basis_v, bas, proj, first_v, second_v, part_refs,
    send_sem, recv_sem, load_sem,
):
    dp, fs = lax.axis_index("dp"), lax.axis_index("fsdp")
    zh, xy = lax.rem(dp, Z_HI), dp // Z_HI
    x, y = lax.rem(xy, X), xy // X
    core, zl = lax.rem(fs, CORES), fs // CORES
    z = zh * Z_LO + zl
    half_tokens = tok_v.shape[0]
    deep = bas.shape[4]
    rows = basis_v.shape[1]
    cols = grad.shape[0]

    def device(y_, x_, z_, core_):
        return ((y_ * X + x_) * Z_HI + z_ // Z_LO, lax.rem(z_, Z_LO) * CORES + core_)

    at_y = lambda t: device(t, x, z, core)
    at_x = lambda t: device(y, t, z, core)
    at_z = lambda t: device(y, x, t, core)
    opposite = wrap(z + Z_LO - RING, RING)
    sibling = device(y, x, z, 1 - core)
    partner = at_z(opposite)

    sent = []

    def send(src, dst, target):
        k = len(sent)
        copy = pltpu.make_async_remote_copy(
            src_ref=src, dst_ref=dst, send_sem=send_sem.at[k], recv_sem=recv_sem.at[k],
            device_id=target, device_id_type=MESH,
        )
        copy.start()
        sent.append(copy)
        return copy

    def ring_gather(n, pos, target, block, half):
        flying = {}
        for s in range(n // 2):
            for d, h in ((1, 0), (-1, 1)):
                t = wrap(pos - d * s, n)
                if s:
                    flying[d].wait_recv()
                ref = block(t) if s < n // 2 - 1 else half(t, h)
                flying[d] = send(ref, ref, target(wrap(pos + d, n)))
            yield
        for copy in flying.values():
            copy.wait_recv()

    def ring_scatter(pos, target, own, sbuf, rbuf, result):
        size = own.shape[1] // 2
        halves = (pl.ds(0, size), pl.ds(size, size))
        far, first_half, second_half = wrap(pos + 2 - X, X), {}, {}
        for i, d in ((0, 1), (1, -1)):
            t = wrap(pos + d, X)
            mine, other = halves[i], halves[1 - i]
            sbuf[i, 0, mine] = own[far, mine].astype(BF16)
            first_half[i] = send(sbuf.at[i, 0, mine], rbuf.at[i, 0, mine], target(t))
            sbuf[i, 1, other] = own[t, other].astype(BF16)
            second_half[i] = send(sbuf.at[i, 1, other], rbuf.at[i, 1, other], target(t))
        yield
        for i, d in ((0, 1), (1, -1)):
            t, mine = wrap(pos + d, X), halves[i]
            first_half[i].wait_recv()
            sbuf[i, 1, mine] = (own[t, mine] + rbuf[i, 0, mine].astype(F32)).astype(BF16)
            first_half[i] = send(sbuf.at[i, 1, mine], rbuf.at[i, 1, mine], target(t))
        yield
        total = own[pos]
        for i in (0, 1):
            second_half[i].wait_recv()
            first_half[i].wait_recv()
            total = total + rbuf[i, 1].astype(F32)
        result[...] = total

    def direct_gather(n, pos, target, block):
        flying = []
        for k in nearest(n):
            flying.append(send(block(pos), block(pos), target(wrap(pos + k, n))))
        yield
        for copy in flying:
            copy.wait_recv()

    def direct_scatter(n, pos, target, own, sbuf, rbuf, result):
        flying = []
        for i, k in enumerate(nearest(n)):
            t = wrap(pos + k, n)
            sbuf[i] = own[t].astype(BF16)
            flying.append(send(sbuf.at[i], rbuf.at[i], target(t)))
        yield
        total = own[pos]
        for i, copy in enumerate(flying):
            copy.wait_recv()
            total = total + rbuf[i].astype(F32)
        result[...] = total.reshape(result.shape)

    loads = [
        pltpu.make_async_copy(basis, basis_v.at[zh], load_sem.at[0]),
        pltpu.make_async_copy(first, first_v.at[zh], load_sem.at[1]),
        pltpu.make_async_copy(second, second_v.at[zh], load_sem.at[2]),
        pltpu.make_async_copy(tokens.at[pl.ds(core * half_tokens, half_tokens)], tok_v, load_sem.at[3]),
        pltpu.make_async_copy(grad, grad_v, load_sem.at[4]),
    ]
    for load in loads:
        load.start()

    barrier = pltpu.get_barrier_semaphore()
    near = [at_z(wrap(z + k - RING, RING)) for k in range(1, RING)] + [sibling]
    near += [at_x(wrap(x + k, X)) for k in nearest(X)]
    for k in nearest(Y):
        t = wrap(y + k, Y)
        near += [at_y(t), device(t, x, opposite, core)]
    for target in near:
        pl.semaphore_signal(barrier, inc=1, device_id=target, device_id_type=MESH)

    loads[0].wait()
    share = pl.ds(core * (rows // 2), rows // 2)
    bas[y, x, zh, share] = basis_v[zh, share, pl.ds(zl * deep, deep)]
    pl.semaphore_wait(barrier, len(near))
    ref = bas.at[y, x, zh, share]
    columns = {0: [send(ref, ref, partner)]}
    for k in nearest(Y):
        t = wrap(y + k, Y)
        columns[k] = [send(ref, ref, at_y(t)), send(ref, ref, device(t, x, opposite, core))]
    across = {}
    for k in columns:
        for copy in columns[k]:
            copy.wait_recv()
        ref = bas.at[wrap(y - k, Y), x, :, share]
        across[k] = [send(ref, ref, at_x(wrap(x + j, X))) for j in nearest(X)]
    loads[1].wait()
    loads[2].wait()
    to_sibling = {}
    for k in across:
        for copy in across[k]:
            copy.wait_recv()
        ref = bas.at[wrap(y - k, Y), :, :, share]
        to_sibling[k] = send(ref, ref, sibling)

    loads[3].wait()
    inner = X * Z_HI * rows
    total = jnp.zeros((half_tokens, deep), F32)
    for k in to_sibling:
        to_sibling[k].wait_recv()
        t = wrap(y - k, Y)
        total += jnp.dot(
            tok_v[:, pl.ds(pl.multiple_of(t * inner, inner), inner)], bas[t].reshape(inner, deep),
            preferred_element_type=F32,
        )
    mine = pl.ds(core * half_tokens, half_tokens)
    proj[zl, mine] = total.astype(BF16)
    ref = proj.at[zl, mine]
    along = [send(ref, ref, at_z(zh * Z_LO + wrap(zl + k - Z_LO, Z_LO))) for k in range(1, Z_LO)]
    beside = [send(ref, ref, sibling)]
    loads[4].wait()
    for k in range(Z_LO):
        r = wrap(zl - k, Z_LO)
        if k:
            along[k - 1].wait_recv()
            ref = proj.at[r, mine]
            beside.append(send(ref, ref, sibling))
        beside[k].wait_recv()
        turned = proj[r].T
        for (low, width), refs in zip(PARTS, part_refs, strict=True):
            own = refs[0]
            part = lax.dot_general(
                turned, grad_v[pl.ds(low, width)], (((1,), (1,)), ((), ())), preferred_element_type=F32
            )
            high = own.shape[2]
            per = deep // (X * high)
            part = part.reshape(per, X, high, width)
            for t in range(X):
                own[t, pl.ds(r * per, per)] = part[:, t]

    pairs = [send(ref, ref, partner) for ref in (first_v.at[zh], second_v.at[zh], basis_v.at[zh])]
    waiting = list(pairs)

    def column_part(number):
        low, width = PARTS[number]
        own, sbuf, rbuf, mid, sbuf2, rbuf2, total, pair_s, pair_r, whole, out_s, out_r = part_refs[number]
        for _ in range(number * LAG):
            yield
        yield from ring_scatter(x, at_x, own, sbuf, rbuf, mid)
        yield from direct_scatter(Y, y, at_y, mid, sbuf2, rbuf2, total)
        pair_s[...] = total[...].astype(BF16)
        copy = send(pair_s, pair_r, partner)
        yield
        copy.wait_recv()
        while waiting:
            waiting.pop().wait_recv()
        low_grad = total[...] + pair_r[...].astype(F32)
        span = pl.ds(low, width)
        old_first = first_v[:, :, span].reshape(low_grad.shape)
        old_second = second_v[:, :, span].reshape(low_grad.shape)
        fresh_first = beta_one * old_first + (1.0 - beta_one) * low_grad
        fresh_second = beta_two * old_second + (1.0 - beta_two) * low_grad * low_grad
        direction = (
            fresh_first / correct_one / (jnp.sqrt(fresh_second / correct_two) + 1e-08)
        ).astype(BF16)
        whole[y, x] = direction
        below = new_first.shape[0]
        new_first[:, span] = jnp.where(zh == 0, fresh_first[:below], fresh_first[below:])
        new_second[:, span] = jnp.where(zh == 0, fresh_second[:below], fresh_second[below:])
        yield from direct_gather(Y, y, at_y, lambda t: whole.at[t, x])
        yield from ring_gather(
            X, x, at_x, lambda t: whole.at[:, t],
            lambda t, h: whole.at[pl.ds(h * (Y // 2), Y // 2), t],
        )
        block = jnp.dot(
            basis_v[...].reshape(Z_HI * rows, -1), whole[...].reshape(-1, width),
            preferred_element_type=F32,
        ).astype(BF16)
        out_s[...] = block.reshape(out_s.shape)
        moving = {}
        for step in (1, -1):
            to = wrap(z + step, RING)
            moving[step] = send(out_s.at[to // Z_LO], out_r.at[zl, core], at_z(to))
        for step in (2, -2):
            to = wrap(z + step, RING)
            cut = pl.ds(0 if step > 0 else rows // 2, rows // 2)
            moving[step] = send(out_s.at[to // Z_LO, cut], out_r.at[zl, core, cut], at_z(to))
        out_r[zl, core] = out_s[zh]
        beside = [send(out_r.at[zl, core], out_r.at[zl, core], sibling)]
        yield
        for step in (1, -1):
            moving[step].wait_recv()
            ref = out_r.at[wrap(zl - step, Z_LO), core]
            beside.append(send(ref, ref, sibling))
        yield
        moving[2].wait_recv()
        moving[-2].wait_recv()
        ref = out_r.at[wrap(zl + 2, Z_LO), core]
        beside.append(send(ref, ref, sibling))
        yield
        for copy in beside:
            copy.wait_recv()
        for block in range(Z_LO):
            for c in range(CORES):
                at = (block * CORES + c) * cols + low
                update[:, at : at + width] = out_r[block, c]

    interleave(*[column_part(number) for number in range(len(PARTS))])

    for copy in sent:
        copy.wait_send()


def nearest(n):
    return sorted((k for k in range(1 - n // 2, n // 2 + 1) if k), key=abs)


def part_scratch(Y, rank, rows, pair_rows, width):
    block = (Y, pair_rows, width)
    bulk = [((X, *block), F32)] + [((2, 2, *block), BF16)] * 2
    rest = [(block, F32)] + [((Y - 1, pair_rows, width), BF16)] * 2
    return bulk + rest + [
        ((pair_rows, width), F32),
        ((pair_rows, width), BF16),
        ((pair_rows, width), BF16),
        ((Y, X, pair_rows, width), BF16),
        ((Z_HI, rows, width), BF16),
        ((Z_LO, CORES, rows, width), BF16),
    ]


def on_device(Y, tokens, grad, basis, first, second):
    held, width = tokens.shape
    cols = grad.shape[1]
    rows, rank = basis.shape
    own = first.shape[0]
    deep = rank // Z_LO
    scratch = [
        ((held // 2, width), BF16),
        ((cols, held), BF16),
        ((Z_HI, rows, rank), BF16),
        ((Y, X, Z_HI, rows, deep), BF16),
        ((Z_LO, held, deep), BF16),
        ((Z_HI, own, cols), F32),
        ((Z_HI, own, cols), F32),
        [part_scratch(Y, rank, rows, Z_HI * own, wide) for _, wide in PARTS],
    ]

    def placed(item):
        return [placed(one) for one in item] if isinstance(item, list) else pltpu.VMEM(*item)

    return pl.pallas_call(
        functools.partial(kernel, Y),
        out_shape=(
            jax.ShapeDtypeStruct(first.shape, F32),
            jax.ShapeDtypeStruct(second.shape, F32),
            jax.ShapeDtypeStruct((rows, Z_LO * CORES * cols), BF16),
        ),
        in_specs=[pl.BlockSpec(memory_space=pltpu.HBM)] * 5,
        out_specs=(pl.BlockSpec(memory_space=pltpu.VMEM),) * 3,
        scratch_shapes=placed(scratch)
        + [
            pltpu.SemaphoreType.DMA((COPIES,)),
            pltpu.SemaphoreType.DMA((COPIES,)),
            pltpu.SemaphoreType.DMA((5,)),
        ],
        compiler_params=pltpu.CompilerParams(
            collective_id=0, has_side_effects=True, vmem_limit_bytes=51 * 2**20
        ),
        cost_estimate=pl.CostEstimate(flops=2 * 10**9, bytes_accessed=10**7, transcendentals=0),
    )(tokens, grad.T, basis, first, second)


def solution(mesh):
    placed = (P("dp", None), P("dp", "fsdp"), P("dp", None), P("dp", "fsdp"), P("dp", "fsdp"))
    Y = mesh.shape["dp"] // (X * Z_HI)
    return jax.shard_map(
        functools.partial(on_device, Y),
        mesh=mesh,
        in_specs=placed,
        out_specs=(P("dp", "fsdp"), P("dp", "fsdp"), P("dp", None)),
        check_vma=False,
    )
```

time: 1210 us -> 106 us (0.09)
  waiting for transfers between devices: 1180 us -> 0 us
  Pallas kernels: 0 us -> 99.5 us
  between operations: 14.4 us -> 0.65 us
    unnamed x5 -> x0, waiting for transfers between devices: 805 us -> none
    all_gather x3 -> x0, waiting for transfers between devices: 373 us -> none  [the longest x1 172 us: on_device(): lax.all_gather(direction, 'dp', axis=0, tiled=True)]
    pallas_call x0 -> x1, Pallas kernels: none -> 99.5 us  [on_device(): pl.pallas_call(functools.partial(kernel, Y), out_shape=(jax.ShapeDtypeStr...]
  transfers between devices with their start and end apart: 4 -> 0, of which waited for: 4 -> 0; matrix products, arithmetic and copies ran while one was open for 0% -> 0% of each run, Pallas kernels for 0% -> 0%
where the time goes in v2:
time: 106 us
  Pallas kernels  99.5 us (94%)
  local copies, waits for them, and re-layouts  5.96 us (6%)
    pallas_call x1, Pallas kernels, on_device(): pl.pallas_call(functools.partial(kernel, Y), out_shape=(jax.ShapeDtypeStr...  99.5 us
    unnamed x11, local copies, waits for them, and re-layouts  5.96 us

profile of v2, /device:TPU:1, one launch (start us, length us, event | category | flops | bytes accessed | tf_op | source)
XLA Modules:
  0.0 106.1 jit_solution(16892492899623536856)
XLA Ops:
  0.6 0.0 copy-start
  0.6 1.2 %copy-done = bf16[384,1376]{0,1:T(8,128)(2,1)S(1)} copy-done((bf16[384,1376]{0,1:T(8,128)(2,1)S(1)}, bf16[384,1376]{0,1:T(8,128)(2,1)}, u32[]{:S(2)}) %copy-start) | copy-done | bytes 1056792
  1.9 0.0 copy-start.1
  1.9 0.8 copy-done.1
  2.7 0.0 copy-start.2
  2.7 0.8 copy-done.2
  3.5 0.0 copy-start.3
  3.5 0.8 copy-done.3
  4.3 99.5 %shard_map.76 = (f32[8,1376]{1,0:T(8,128)S(1)}, f32[8,1376]{1,0:T(8,128)S(1)}, bf16[64,11008]{1,0:T(8,128)(2,1)S(1)}) custom-call(bf16[384,4096]{1,0:T(8,128)(2,1)} %tokens.1, bf16[1376,384]{1,0:T(8,128)(2,1)S(1)} %bitcast.1, bf16[64,512]{1,0:T(8,128)(2,1)S(1)} %copy-done.1, f32[8,1376]{1,0:T(8,128)S(1)} %copy-done.2, f32[8,1376]{1,0:T(8,128)S(1)} %copy-done.3), custom_call_target="tpu_custom_call" | custom-call | flops 2000000000 | bytes 10000000 | tf_op jit(solution)/shard_map/pallas_call | solution.py:322
  103.8 0.6 copy.11
  104.4 0.6 copy.12
  105.0 1.1 %copy.13 = bf16[64,11008]{1,0:T(8,128)(2,1)} copy(bf16[64,11008]{1,0:T(8,128)(2,1)S(1)} %get-tuple-element.8) | data formatting | bytes 2818048
Async XLA Ops:
  0.6 1.2 %copy-start = (bf16[384,1376]{0,1:T(8,128)(2,1)S(1)}, bf16[384,1376]{0,1:T(8,128)(2,1)}, u32[]{:S(2)}) copy-start(bf16[384,1376]{0,1:T(8,128)(2,1)} %param.6) | copy-start | bytes 3170308
  1.9 0.8 copy-start.1
  2.7 0.8 copy-start.2
  3.5 0.8 copy-start.3

commit v3 on v2

v3 whole, which is shorter than its diff:
```python
import functools
import itertools

import jax
import jax.numpy as jnp
from jax import lax
from jax.experimental import pallas as pl
from jax.experimental.pallas import tpu as pltpu
from jax.sharding import PartitionSpec as P

beta_one = 0.9
beta_two = 0.999
correct_one = 1.0 - 0.9**10
correct_two = 1.0 - 0.999**10

X = 4
Z_HI, Z_LO, CORES = 2, 4, 2
RING = Z_HI * Z_LO
PARTS = ((0, 512, "y"), (512, 512, "x"), (1024, 352, "x"))
COPIES = 67

MESH = pl.DeviceIdType.MESH
F32, BF16 = jnp.float32, jnp.bfloat16


def wrap(value, n):
    return lax.rem(value + n, n)


def interleave(*steps):
    steps = list(steps)
    while steps:
        steps = [step for step in steps if next(step, "end") != "end"]


def kernel(
    Y, tokens, grad, basis, first, second,
    own_grad, blocks,
    tok_v, grad_v, basis_v, bas, proj, first_v, second_v, grad_sum,
    own, sbuf, rbuf, mid, row_s, row_r, pair_s, pair_r, part_refs,
    send_sem, recv_sem, load_sem,
):
    dp, fs = lax.axis_index("dp"), lax.axis_index("fsdp")
    zh, xy = lax.rem(dp, Z_HI), dp // Z_HI
    x, y = lax.rem(xy, X), xy // X
    core, zl = lax.rem(fs, CORES), fs // CORES
    z = zh * Z_LO + zl
    half_tokens = tok_v.shape[0]
    deep = bas.shape[4]
    rows = basis_v.shape[1]
    cols = grad.shape[0]

    def device(y_, x_, z_, core_):
        return ((y_ * X + x_) * Z_HI + z_ // Z_LO, lax.rem(z_, Z_LO) * CORES + core_)

    at_y = lambda t: device(t, x, z, core)
    at_x = lambda t: device(y, t, z, core)
    at_z = lambda t: device(y, x, t, core)
    opposite = wrap(z + Z_LO - RING, RING)
    sibling = device(y, x, z, 1 - core)
    partner = at_z(opposite)

    sent, lanes = [], itertools.count()

    def send(src, dst, target, lane=None):
        k = next(lanes) if lane is None else lane
        copy = pltpu.make_async_remote_copy(
            src_ref=src, dst_ref=dst, send_sem=send_sem.at[k], recv_sem=recv_sem.at[k],
            device_id=target, device_id_type=MESH,
        )
        copy.start()
        if lane is None:
            sent.append(copy)
        return copy

    def joint(lane, whole):
        copy = pltpu.make_async_remote_copy(
            src_ref=whole, dst_ref=whole, send_sem=send_sem.at[lane], recv_sem=recv_sem.at[lane],
            device_id=sibling, device_id_type=MESH,
        )
        sent.append(copy)
        return copy

    def ring_gather(n, pos, target, block, half):
        flying = [send(block(pos), block(pos), target(wrap(pos + d, n))) for d in (1, -1)]
        for s in range(1, n // 2):
            yield
            if n == X:
                yield
            lane = next(lanes) if s == n // 2 - 1 else None
            for i, d in ((0, 1), (1, -1)):
                flying[i].wait_recv()
                t = wrap(pos - d * s, n)
                if s < n // 2 - 1:
                    flying[i] = send(block(t), block(t), target(wrap(pos + d, n)))
                else:
                    send(half(t, i), half(t, i), target(wrap(pos + d, n)), lane)
        both = joint(lane, block(wrap(pos + n // 2 - n, n)))
        yield
        both.wait_recv()

    def direct_scatter(pos, target, own, sbuf, rbuf, result):
        lane = next(lanes)
        for i, k in enumerate(nearest(X)):
            t = wrap(pos + k, X)
            sbuf[i] = own[t].astype(BF16)
            send(sbuf.at[i], rbuf.at[i], target(t), lane)
        every = joint(lane, rbuf)
        yield
        total = own[pos]
        every.wait_recv()
        for i in range(X - 1):
            total = total + rbuf[i].astype(F32)
        result[...] = total

    def direct_gather(n, pos, target, block, others):
        lane = next(lanes)
        for k in nearest(n):
            send(block(pos), block(pos), target(wrap(pos + k, n)), lane)
        every = joint(lane, others)
        yield
        if n == Y:
            yield
        every.wait_recv()

    loads = [
        pltpu.make_async_copy(basis, basis_v.at[zh], load_sem.at[0]),
        pltpu.make_async_copy(first, first_v.at[zh], load_sem.at[1]),
        pltpu.make_async_copy(second, second_v.at[zh], load_sem.at[2]),
        pltpu.make_async_copy(tokens.at[pl.ds(core * half_tokens, half_tokens)], tok_v, load_sem.at[3]),
        pltpu.make_async_copy(grad, grad_v, load_sem.at[4]),
    ]
    for load in loads:
        load.start()

    barrier = pltpu.get_barrier_semaphore()
    near = [at_z(wrap(z + k - RING, RING)) for k in range(1, RING)] + [sibling]
    near += [at_x(wrap(x + k, X)) for k in nearest(X)]
    for k in nearest(Y):
        t = wrap(y + k, Y)
        near += [at_y(t), device(t, x, opposite, core)]
    for target in near:
        pl.semaphore_signal(barrier, inc=1, device_id=target, device_id_type=MESH)

    loads[0].wait()
    share = pl.ds(core * (rows // 2), rows // 2)
    rank, y_rows = basis_v.shape[2], basis_v.shape[2] // Y
    column = lax.broadcasted_iota(jnp.int32, (rank, deep), 1)
    wanted = (zl + Z_LO * (column // y_rows)) * y_rows + lax.rem(column, y_rows)
    picks = (lax.broadcasted_iota(jnp.int32, (rank, deep), 0) == wanted).astype(BF16)
    bas[y, x, zh, share] = jnp.dot(
        basis_v[zh, share], picks, preferred_element_type=F32
    ).astype(BF16)
    pl.semaphore_wait(barrier, len(near))
    ref = bas.at[y, x, zh, share]
    columns = {0: send(ref, ref, partner)}
    for k in nearest(Y):
        t = wrap(y + k, Y)
        lane = next(lanes)
        send(ref, ref, at_y(t), lane)
        send(ref, ref, device(t, x, opposite, core), lane)
        columns[k] = joint(lane, bas.at[t, x, :, share])
    across = {}
    for k in columns:
        columns[k].wait_recv()
        ref = bas.at[wrap(y - k, Y), x, :, share]
        lane = next(lanes)
        for j in nearest(X):
            send(ref, ref, at_x(wrap(x + j, X)), lane)
        across[k] = joint(lane, bas.at[wrap(y - k, Y), pl.ds(0, X - 1), :, share])
    to_sibling = {}
    for k in across:
        across[k].wait_recv()
        ref = bas.at[wrap(y - k, Y), :, :, share]
        to_sibling[k] = send(ref, ref, sibling)

    loads[3].wait()
    inner = X * Z_HI * rows
    total = jnp.zeros((half_tokens, deep), F32)
    for k in to_sibling:
        to_sibling[k].wait_recv()
        t = wrap(y - k, Y)
        total += jnp.dot(
            tok_v[:, pl.ds(pl.multiple_of(t * inner, inner), inner)], bas[t].reshape(inner, deep),
            preferred_element_type=F32,
        )
    mine = pl.ds(core * half_tokens, half_tokens)
    proj[zl, mine] = total.astype(BF16)
    ref = proj.at[zl, mine]
    along = [next(lanes) for _ in range(1, Z_LO)]
    for k in range(1, Z_LO):
        send(ref, ref, at_z(zh * Z_LO + wrap(zl + k - Z_LO, Z_LO)), along[k - 1])
    for lane in along:
        joint(lane, ref)
    beside = [send(ref, ref, sibling)]
    loads[4].wait()
    high = own.shape[3]
    per = deep // (X * high)
    row_lane = next(lanes)

    def rank_slice(k, r):
        yield from direct_scatter(x, at_x, own.at[k], sbuf.at[k], rbuf.at[k], mid.at[r])
        for j in range(per):
            t = r + j * Z_LO
            row_s[t] = mid[r, j].astype(BF16)

            @pl.when(t != y)
            def _():
                send(row_s.at[t], row_r.at[y], at_y(t), row_lane)

    def advance(steps):
        steps[:] = [step for step in steps if next(step, "end") != "end"]

    summing = []
    for k in range(Z_LO):
        r = zl
        if k:
            far = 1 + lax.rem(k - 1 + y, Z_LO - 1)
            r = wrap(zl - far, Z_LO)
            ref = proj.at[r, mine]
            pltpu.make_async_remote_copy(
                src_ref=ref, dst_ref=ref, send_sem=send_sem.at[along[0] + far - 1],
                recv_sem=recv_sem.at[along[0] + far - 1], device_id=sibling, device_id_type=MESH,
            ).wait_recv()
            beside.append(send(ref, ref, sibling))
        beside[k].wait_recv()
        part = lax.dot_general(
            proj[r].T, grad_v[...], (((1,), (1,)), ((), ())), preferred_element_type=F32
        ).reshape(per, X, high, cols)
        for t in range(X):
            own[k, t] = part[:, t]
        summing.insert(0, rank_slice(k, r))
        advance(summing)
    loads[1].wait()
    loads[2].wait()
    lane = next(lanes)
    for ref in (first_v.at[zh], second_v.at[zh]):
        send(ref, ref, partner, lane)
    moments = joint(lane, first_v)
    while summing:
        advance(summing)
    row_sums = joint(row_lane, row_r.at[pl.ds(0, Y - 1)])

    total = mid[lax.rem(y, Z_LO), y // Z_LO]
    row_sums.wait_recv()
    for k in nearest(Y):
        total = total + row_r[wrap(y + k, Y)].astype(F32)
    pair_s[...] = total.astype(BF16)
    copy = send(pair_s, pair_r, partner)
    basis_pair = [send(basis_v.at[zh], basis_v.at[zh], partner)]
    moments.wait_recv()
    copy.wait_recv()
    low_grad = total + pair_r[...].astype(F32)
    fresh_first = beta_one * first_v[...].reshape(low_grad.shape) + (1.0 - beta_one) * low_grad
    fresh_second = (
        beta_two * second_v[...].reshape(low_grad.shape) + (1.0 - beta_two) * low_grad * low_grad
    )
    direction = (
        fresh_first / correct_one / (jnp.sqrt(fresh_second / correct_two) + 1e-08)
    ).astype(BF16)
    below = grad_sum.shape[0]
    grad_sum[...] = jnp.where(zh == 0, low_grad[:below], low_grad[below:])
    store = pltpu.make_async_copy(grad_sum, own_grad, load_sem.at[5 + len(PARTS)])
    store.start()
    stores = [store]
    for (low, width, _), refs in zip(PARTS, part_refs, strict=True):
        refs[0][y, x] = direction[:, low : low + width]

    def column_part(number):
        low, width, way = PARTS[number]
        whole, out_s, out_r = part_refs[number]
        if way == "y":
            yield from direct_gather(
                X, x, at_x, lambda t: whole.at[y, t], whole.at[y, pl.ds(0, X - 1)]
            )
            yield from ring_gather(
                Y, y, at_y, lambda t: whole.at[t],
                lambda t, h: whole.at[t, pl.ds(h * (X // 2), X // 2)],
            )
        else:
            yield from direct_gather(
                Y, y, at_y, lambda t: whole.at[t, x], whole.at[pl.ds(0, Y - 1), x]
            )
            yield from ring_gather(
                X, x, at_x, lambda t: whole.at[:, t],
                lambda t, h: whole.at[pl.ds(h * (Y // 2), Y // 2), t],
            )
        while basis_pair:
            basis_pair.pop().wait_recv()
        block = jnp.dot(
            basis_v[...].reshape(Z_HI * rows, -1), whole[...].reshape(-1, width),
            preferred_element_type=F32,
        ).astype(BF16)
        out_s[...] = block.reshape(out_s.shape)
        moving = {}
        for step in (1, -1):
            to = wrap(z + step, RING)
            moving[step] = send(out_s.at[to // Z_LO], out_r.at[zl, core], at_z(to))
        lane = next(lanes)
        for step in (2, -2):
            to = wrap(z + step, RING)
            cut = pl.ds(0 if step > 0 else rows // 2, rows // 2)
            send(out_s.at[to // Z_LO, cut], out_r.at[zl, core, cut], at_z(to), lane)
        far = out_r.at[wrap(zl + 2 - Z_LO, Z_LO), core]
        moving[2] = joint(lane, far)
        out_r[zl, core] = out_s[zh]
        lane = next(lanes)
        send(out_r.at[zl, core], out_r.at[zl, core], sibling, lane)
        yield
        for step in (1, -1):
            moving[step].wait_recv()
            ref = out_r.at[wrap(zl - step, Z_LO), core]
            send(ref, ref, sibling, lane)
        yield
        moving[2].wait_recv()
        send(far, far, sibling, lane)
        beside = joint(lane, out_r.at[:, 1 - core])
        yield
        beside.wait_recv()
        store = pltpu.make_async_copy(out_r, blocks[number], load_sem.at[5 + number])
        store.start()
        stores.append(store)

    interleave(*[column_part(number) for number in range(len(PARTS))])
    used = next(lanes)
    assert used == COPIES, used

    for copy in sent:
        copy.wait_send()
    for store in stores:
        store.wait()


def finish(own_grad, first, second, blocks, new_first, new_second, update):
    low_grad = own_grad[...]
    new_first[...] = beta_one * first[...] + (1.0 - beta_one) * low_grad
    new_second[...] = beta_two * second[...] + (1.0 - beta_two) * low_grad * low_grad
    cols = first.shape[1]
    for (low, width, _), part in zip(PARTS, blocks, strict=True):
        for block in range(Z_LO):
            for c in range(CORES):
                at = (block * CORES + c) * cols + low
                update[:, at : at + width] = part[block, c]


def nearest(n):
    return sorted((k for k in range(1 - n // 2, n // 2 + 1) if k), key=abs)


def on_device(Y, tokens, grad, basis, first, second):
    held, width = tokens.shape
    cols = grad.shape[1]
    rows, rank = basis.shape
    own = first.shape[0]
    deep = rank // Z_LO
    per, pair_rows = Y // Z_LO, Z_HI * own
    scratch = [
        ((held // 2, width), BF16),
        ((cols, held), BF16),
        ((Z_HI, rows, rank), BF16),
        ((Y, X, Z_HI, rows, deep), BF16),
        ((Z_LO, held, deep), BF16),
        ((Z_HI, own, cols), F32),
        ((Z_HI, own, cols), F32),
        ((own, cols), F32),
        ((Z_LO, X, per, pair_rows, cols), F32),
        ((Z_LO, X - 1, per, pair_rows, cols), BF16),
        ((Z_LO, X - 1, per, pair_rows, cols), BF16),
        ((Z_LO, per, pair_rows, cols), F32),
        ((Y, pair_rows, cols), BF16),
        ((Y, pair_rows, cols), BF16),
        ((pair_rows, cols), BF16),
        ((pair_rows, cols), BF16),
        [
            [
                ((Y, X, pair_rows, wide), BF16),
                ((Z_HI, rows, wide), BF16),
                ((Z_LO, CORES, rows, wide), BF16),
            ]
            for _, wide, _ in PARTS
        ],
    ]

    def placed(item):
        return [placed(one) for one in item] if isinstance(item, list) else pltpu.VMEM(*item)

    placed_blocks = [jax.ShapeDtypeStruct((Z_LO, CORES, rows, wide), BF16) for _, wide, _ in PARTS]
    anywhere = pl.BlockSpec(memory_space=pl.ANY)
    own_grad, blocks = pl.pallas_call(
        functools.partial(kernel, Y),
        out_shape=(jax.ShapeDtypeStruct(first.shape, F32), placed_blocks),
        in_specs=[anywhere] * 5,
        out_specs=(anywhere, [anywhere] * len(PARTS)),
        scratch_shapes=placed(scratch)
        + [
            pltpu.SemaphoreType.DMA((COPIES,)),
            pltpu.SemaphoreType.DMA((COPIES,)),
            pltpu.SemaphoreType.DMA((6 + len(PARTS),)),
        ],
        compiler_params=pltpu.CompilerParams(
            collective_id=0, has_side_effects=True, vmem_limit_bytes=56 * 2**20
        ),
        cost_estimate=pl.CostEstimate(flops=2 * 10**9, bytes_accessed=10**7, transcendentals=0),
    )(tokens, grad.T, basis, first, second)
    high = 16
    whole = pl.BlockSpec(first.shape, lambda i: (0, 0))
    return pl.pallas_call(
        finish,
        grid=(rows // high,),
        out_shape=(
            jax.ShapeDtypeStruct(first.shape, F32),
            jax.ShapeDtypeStruct(second.shape, F32),
            jax.ShapeDtypeStruct((rows, Z_LO * CORES * cols), BF16),
        ),
        in_specs=[
            whole, whole, whole,
            [pl.BlockSpec((Z_LO, CORES, high, wide), lambda i: (0, 0, i, 0)) for _, wide, _ in PARTS],
        ],
        out_specs=(whole, whole, pl.BlockSpec((high, Z_LO * CORES * cols), lambda i: (i, 0))),
        compiler_params=pltpu.CompilerParams(vmem_limit_bytes=56 * 2**20),
        cost_estimate=pl.CostEstimate(flops=10**5, bytes_accessed=3 * 10**6, transcendentals=0),
    )(own_grad, first, second, blocks)


def solution(mesh):
    placed = (P("dp", None), P("dp", "fsdp"), P("dp", None), P("dp", "fsdp"), P("dp", "fsdp"))
    Y = mesh.shape["dp"] // (X * Z_HI)
    return jax.shard_map(
        functools.partial(on_device, Y),
        mesh=mesh,
        in_specs=placed,
        out_specs=(P("dp", "fsdp"), P("dp", "fsdp"), P("dp", None)),
        check_vma=False,
    )
```

time: 106 us -> 96.9 us (0.914)
  local copies, waits for them, and re-layouts: 5.96 us -> 0 us
  Pallas kernels: 99.5 us -> 96 us
    pallas_call x1, Pallas kernels: 99.5 us -> 92.2 us  [on_device(): pl.pallas_call(functools.partial(kernel, Y), out_shape=(jax.ShapeDtypeStr...]
    unnamed x11 -> x0, local copies, waits for them, and re-layouts: 5.96 us -> none
    pallas_call x0 -> x1, Pallas kernels: none -> 3.87 us  [on_device(): pl.pallas_call(finish, grid=(rows // high,), out_shape=(jax.ShapeDtypeStr...]
where the time goes in v3:
time: 96.9 us; the launch traced here: 96.7 us
  Pallas kernels  96 us (99%)
    pallas_call x1, Pallas kernels, on_device(): pl.pallas_call(functools.partial(kernel, Y), out_shape=(jax.ShapeDtypeStr...  92.2 us
    pallas_call x1, Pallas kernels, on_device(): pl.pallas_call(finish, grid=(rows // high,), out_shape=(jax.ShapeDtypeStr...  3.87 us

profile of v3, /device:TPU:1, one launch (start us, length us, event | category | flops | bytes accessed | tf_op | source)
XLA Modules:
  0.0 96.7 jit_solution(7813628699255794812)
XLA Ops:
  0.6 92.2 %shard_map.76 = (f32[8,1376]{1,0:T(8,128)}, bf16[4,2,64,512]{3,2,1,0:T(8,128)(2,1)}, bf16[4,2,64,512]{3,2,1,0:T(8,128)(2,1)}, bf16[4,2,64,352]{3,2,1,0:T(8,128)(2,1)}) custom-call(bf16[384,4096]{1,0:T(8,128)(2,1)} %tokens.1, bf16[1376,384]{1,0:T(8,128)(2,1)} %bitcast.1, bf16[64,512]{1,0:T(8,128)(2,1)} %basis.1, f32[8,1376]{1,0:T(8,128)} %first.3, ...), custom_call_target="tpu_custom_call" | custom-call | flops 2000000000 | bytes 10000000 | tf_op jit(solution)/shard_map/pallas_call | solution.py:389
  92.8 3.9 %shard_map.77 = (f32[8,1376]{1,0:T(8,128)}, f32[8,1376]{1,0:T(8,128)}, bf16[64,11008]{1,0:T(8,128)(2,1)}) custom-call(f32[8,1376]{1,0:T(8,128)} %get-tuple-element.7.own_grad, f32[8,1376]{1,0:T(8,128)} %first.3, f32[8,1376]{1,0:T(8,128)} %second.3, bf16[4,2,64,512]{3,2,1,0:T(8,128)(2,1)} %get-tuple-element.8.blocks_0_, ...), custom_call_target="tpu_custom_call" | custom-call | flops 100000 | bytes 3000000 | tf_op jit(solution)/shard_map/pallas_call | solution.py:407

commit v4 on v3

--- a/solution.py
+++ b/solution.py
@@ -208,9 +208,6 @@
             def _():
                 send(row_s.at[t], row_r.at[y], at_y(t), row_lane)
 
-    def advance(steps):
-        steps[:] = [step for step in steps if next(step, "end") != "end"]
-
     summing = []
     for k in range(Z_LO):
         r = zl
@@ -223,22 +220,25 @@
                 recv_sem=recv_sem.at[along[0] + far - 1], device_id=sibling, device_id_type=MESH,
             ).wait_recv()
             beside.append(send(ref, ref, sibling))
+        if k == Z_LO - 1:
+            loads[1].wait()
+            loads[2].wait()
+            lane = next(lanes)
+            for ref in (first_v.at[zh], second_v.at[zh]):
+                send(ref, ref, partner, lane)
+            moments = joint(lane, first_v)
         beside[k].wait_recv()
         part = lax.dot_general(
             proj[r].T, grad_v[...], (((1,), (1,)), ((), ())), preferred_element_type=F32
         ).reshape(per, X, high, cols)
         for t in range(X):
             own[k, t] = part[:, t]
-        summing.insert(0, rank_slice(k, r))
-        advance(summing)
-    loads[1].wait()
-    loads[2].wait()
-    lane = next(lanes)
-    for ref in (first_v.at[zh], second_v.at[zh]):
-        send(ref, ref, partner, lane)
-    moments = joint(lane, first_v)
-    while summing:
-        advance(summing)
+        summing.append(rank_slice(k, r))
+        next(summing[k])
+        if k >= 2:
+            next(summing[k - 2], None)
+    for step in summing[Z_LO - 2 :]:
+        next(step, None)
     row_sums = joint(row_lane, row_r.at[pl.ds(0, Y - 1)])
 
     total = mid[lax.rem(y, Z_LO), y // Z_LO]
@@ -247,9 +247,9 @@
         total = total + row_r[wrap(y + k, Y)].astype(F32)
     pair_s[...] = total.astype(BF16)
     copy = send(pair_s, pair_r, partner)
-    basis_pair = [send(basis_v.at[zh], basis_v.at[zh], partner)]
     moments.wait_recv()
     copy.wait_recv()
+    basis_pair = [send(basis_v.at[zh], basis_v.at[zh], partner)]
     low_grad = total + pair_r[...].astype(F32)
     fresh_first = beta_one * first_v[...].reshape(low_grad.shape) + (1.0 - beta_one) * low_grad
     fresh_second = (
@@ -402,7 +402,7 @@
         ),
         cost_estimate=pl.CostEstimate(flops=2 * 10**9, bytes_accessed=10**7, transcendentals=0),
     )(tokens, grad.T, basis, first, second)
-    high = 16
+    high = 32
     whole = pl.BlockSpec(first.shape, lambda i: (0, 0))
     return pl.pallas_call(
         finish,

time: 96.9 us -> 94.1 us (0.971)
  Pallas kernels: 96 us -> 93.3 us
    pallas_call x1, Pallas kernels: 3.87 us -> 2.47 us  [on_device(): pl.pallas_call(finish, grid=(rows // high,), out_shape=(jax.ShapeDtypeStr...]
    pallas_call x1, Pallas kernels: 92.2 us -> 90.8 us  [on_device(): pl.pallas_call(functools.partial(kernel, Y), out_shape=(jax.ShapeDtypeStr...]
where the time goes in v4:
time: 94.1 us; the launch traced here: 93.9 us
  Pallas kernels  93.3 us (99%)
    pallas_call x1, Pallas kernels, on_device(): pl.pallas_call(functools.partial(kernel, Y), out_shape=(jax.ShapeDtypeStr...  90.8 us
    pallas_call x1, Pallas kernels, on_device(): pl.pallas_call(finish, grid=(rows // high,), out_shape=(jax.ShapeDtypeStr...  2.47 us

profile of v4, /device:TPU:1, one launch (start us, length us, event | category | flops | bytes accessed | tf_op | source)
XLA Modules:
  0.0 93.9 jit_solution(3066287853507999501)
XLA Ops:
  0.6 90.8 %shard_map.76 = (f32[8,1376]{1,0:T(8,128)}, bf16[4,2,64,512]{3,2,1,0:T(8,128)(2,1)}, bf16[4,2,64,512]{3,2,1,0:T(8,128)(2,1)}, bf16[4,2,64,352]{3,2,1,0:T(8,128)(2,1)}) custom-call(bf16[384,4096]{1,0:T(8,128)(2,1)} %tokens.1, bf16[1376,384]{1,0:T(8,128)(2,1)} %bitcast.1, bf16[64,512]{1,0:T(8,128)(2,1)} %basis.1, f32[8,1376]{1,0:T(8,128)} %first.3, ...), custom_call_target="tpu_custom_call" | custom-call | flops 2000000000 | bytes 10000000 | tf_op jit(solution)/shard_map/pallas_call | solution.py:389
  91.4 2.5 %shard_map.77 = (f32[8,1376]{1,0:T(8,128)}, f32[8,1376]{1,0:T(8,128)}, bf16[64,11008]{1,0:T(8,128)(2,1)}) custom-call(f32[8,1376]{1,0:T(8,128)} %get-tuple-element.7.own_grad, f32[8,1376]{1,0:T(8,128)} %first.3, f32[8,1376]{1,0:T(8,128)} %second.3, bf16[4,2,64,512]{3,2,1,0:T(8,128)(2,1)} %get-tuple-element.8.blocks_0_, ...), custom_call_target="tpu_custom_call" | custom-call | flops 100000 | bytes 3000000 | tf_op jit(solution)/shard_map/pallas_call | solution.py:407

commit v5 on v4

--- a/solution.py
+++ b/solution.py
@@ -36,7 +36,7 @@
 def kernel(
     Y, tokens, grad, basis, first, second,
     own_grad, blocks,
-    tok_v, grad_v, basis_v, bas, proj, first_v, second_v, grad_sum,
+    tok_v, grad_v, basis_v, bas, proj, first_v, second_v, grad_sum, turned,
     own, sbuf, rbuf, mid, row_s, row_r, pair_s, pair_r, part_refs,
     send_sem, recv_sem, load_sem,
 ):
@@ -59,6 +59,7 @@
     opposite = wrap(z + Z_LO - RING, RING)
     sibling = device(y, x, z, 1 - core)
     partner = at_z(opposite)
+    mirror = RING - 1 - z
 
     sent, lanes = [], itertools.count()
 
@@ -138,7 +139,7 @@
     near += [at_x(wrap(x + k, X)) for k in nearest(X)]
     for k in nearest(Y):
         t = wrap(y + k, Y)
-        near += [at_y(t), device(t, x, opposite, core)]
+        near += [at_y(t), device(t, x, mirror, core)]
     for target in near:
         pl.semaphore_signal(barrier, inc=1, device_id=target, device_id_type=MESH)
 
@@ -146,19 +147,23 @@
     share = pl.ds(core * (rows // 2), rows // 2)
     rank, y_rows = basis_v.shape[2], basis_v.shape[2] // Y
     column = lax.broadcasted_iota(jnp.int32, (rank, deep), 1)
-    wanted = (zl + Z_LO * (column // y_rows)) * y_rows + lax.rem(column, y_rows)
-    picks = (lax.broadcasted_iota(jnp.int32, (rank, deep), 0) == wanted).astype(BF16)
-    bas[y, x, zh, share] = jnp.dot(
-        basis_v[zh, share], picks, preferred_element_type=F32
-    ).astype(BF16)
+    row = lax.broadcasted_iota(jnp.int32, (rank, deep), 0)
+
+    def slice_of(q):
+        wanted = (q + Z_LO * (column // y_rows)) * y_rows + lax.rem(column, y_rows)
+        picks = (row == wanted).astype(BF16)
+        return jnp.dot(basis_v[zh, share], picks, preferred_element_type=F32).astype(BF16)
+
+    bas[y, x, zh, share] = slice_of(zl)
+    turned[...] = slice_of(Z_LO - 1 - zl)
     pl.semaphore_wait(barrier, len(near))
     ref = bas.at[y, x, zh, share]
-    columns = {0: send(ref, ref, partner)}
+    columns = {0: send(turned, ref, at_z(mirror))}
     for k in nearest(Y):
         t = wrap(y + k, Y)
         lane = next(lanes)
         send(ref, ref, at_y(t), lane)
-        send(ref, ref, device(t, x, opposite, core), lane)
+        send(turned, ref, device(t, x, mirror, core), lane)
         columns[k] = joint(lane, bas.at[t, x, :, share])
     across = {}
     for k in columns:
@@ -363,6 +368,7 @@
         ((Z_HI, own, cols), F32),
         ((Z_HI, own, cols), F32),
         ((own, cols), F32),
+        ((rows // 2, deep), BF16),
         ((Z_LO, X, per, pair_rows, cols), F32),
         ((Z_LO, X - 1, per, pair_rows, cols), BF16),
         ((Z_LO, X - 1, per, pair_rows, cols), BF16),

time: 94.1 us -> 93.2 us (level)
  no operation moved by 1% of the time
where the time goes in v5:
time: 93.2 us; the launch traced here: 93.1 us
  Pallas kernels  92.4 us (99%)
    pallas_call x1, Pallas kernels, on_device(): pl.pallas_call(functools.partial(kernel, Y), out_shape=(jax.ShapeDtypeStr...  90 us
    pallas_call x1, Pallas kernels, on_device(): pl.pallas_call(finish, grid=(rows // high,), out_shape=(jax.ShapeDtypeStr...  2.47 us

profile of v5, /device:TPU:1, one launch (start us, length us, event | category | flops | bytes accessed | tf_op | source)
XLA Modules:
  0.0 93.1 jit_solution(5356626003467209636)
XLA Ops:
  0.6 90.0 %shard_map.76 = (f32[8,1376]{1,0:T(8,128)}, bf16[4,2,64,512]{3,2,1,0:T(8,128)(2,1)}, bf16[4,2,64,512]{3,2,1,0:T(8,128)(2,1)}, bf16[4,2,64,352]{3,2,1,0:T(8,128)(2,1)}) custom-call(bf16[384,4096]{1,0:T(8,128)(2,1)} %tokens.1, bf16[1376,384]{1,0:T(8,128)(2,1)} %bitcast.1, bf16[64,512]{1,0:T(8,128)(2,1)} %basis.1, f32[8,1376]{1,0:T(8,128)} %first.3, ...), custom_call_target="tpu_custom_call" | custom-call | flops 2000000000 | bytes 10000000 | tf_op jit(solution)/shard_map/pallas_call | solution.py:395
  90.6 2.5 %shard_map.77 = (f32[8,1376]{1,0:T(8,128)}, f32[8,1376]{1,0:T(8,128)}, bf16[64,11008]{1,0:T(8,128)(2,1)}) custom-call(f32[8,1376]{1,0:T(8,128)} %get-tuple-element.7.own_grad, f32[8,1376]{1,0:T(8,128)} %first.3, f32[8,1376]{1,0:T(8,128)} %second.3, bf16[4,2,64,512]{3,2,1,0:T(8,128)(2,1)} %get-tuple-element.8.blocks_0_, ...), custom_call_target="tpu_custom_call" | custom-call | flops 100000 | bytes 3000000 | tf_op jit(solution)/shard_map/pallas_call | solution.py:413

commit v6 on v5

--- a/solution.py
+++ b/solution.py
@@ -143,19 +143,24 @@
     for target in near:
         pl.semaphore_signal(barrier, inc=1, device_id=target, device_id_type=MESH)
 
-    loads[0].wait()
     share = pl.ds(core * (rows // 2), rows // 2)
     rank, y_rows = basis_v.shape[2], basis_v.shape[2] // Y
     column = lax.broadcasted_iota(jnp.int32, (rank, deep), 1)
     row = lax.broadcasted_iota(jnp.int32, (rank, deep), 0)
 
-    def slice_of(q):
-        wanted = (q + Z_LO * (column // y_rows)) * y_rows + lax.rem(column, y_rows)
-        picks = (row == wanted).astype(BF16)
-        return jnp.dot(basis_v[zh, share], picks, preferred_element_type=F32).astype(BF16)
-
-    bas[y, x, zh, share] = slice_of(zl)
-    turned[...] = slice_of(Z_LO - 1 - zl)
+    place = Z_LO * (column // y_rows) * y_rows + lax.rem(column, y_rows)
+
+    def picks(q):
+        return (row == place + q * y_rows).astype(BF16)
+
+    own_picks, turned_picks = picks(zl), picks(Z_LO - 1 - zl)
+    loads[0].wait()
+    bas[y, x, zh, share] = jnp.dot(
+        basis_v[zh, share], own_picks, preferred_element_type=F32
+    ).astype(BF16)
+    turned[...] = jnp.dot(
+        basis_v[zh, share], turned_picks, preferred_element_type=F32
+    ).astype(BF16)
     pl.semaphore_wait(barrier, len(near))
     ref = bas.at[y, x, zh, share]
     columns = {0: send(turned, ref, at_z(mirror))}
@@ -298,14 +303,14 @@
         ).astype(BF16)
         out_s[...] = block.reshape(out_s.shape)
         moving = {}
-        for step in (1, -1):
-            to = wrap(z + step, RING)
-            moving[step] = send(out_s.at[to // Z_LO], out_r.at[zl, core], at_z(to))
         lane = next(lanes)
         for step in (2, -2):
             to = wrap(z + step, RING)
             cut = pl.ds(0 if step > 0 else rows // 2, rows // 2)
             send(out_s.at[to // Z_LO, cut], out_r.at[zl, core, cut], at_z(to), lane)
+        for step in (1, -1):
+            to = wrap(z + step, RING)
+            moving[step] = send(out_s.at[to // Z_LO], out_r.at[zl, core], at_z(to))
         far = out_r.at[wrap(zl + 2 - Z_LO, Z_LO), core]
         moving[2] = joint(lane, far)
         out_r[zl, core] = out_s[zh]

time: 93.2 us -> 93.2 us (level)
  no operation moved by 1% of the time
where the time goes in v6:
time: 93.2 us; the launch traced here: 93 us
  Pallas kernels  92.3 us (99%)
    pallas_call x1, Pallas kernels, on_device(): pl.pallas_call(functools.partial(kernel, Y), out_shape=(jax.ShapeDtypeStr...  89.9 us
    pallas_call x1, Pallas kernels, on_device(): pl.pallas_call(finish, grid=(rows // high,), out_shape=(jax.ShapeDtypeStr...  2.47 us

profile of v6, /device:TPU:1, one launch (start us, length us, event | category | flops | bytes accessed | tf_op | source)
XLA Modules:
  0.0 93.0 jit_solution(4900995758711591972)
XLA Ops:
  0.6 89.9 %shard_map.76 = (f32[8,1376]{1,0:T(8,128)}, bf16[4,2,64,512]{3,2,1,0:T(8,128)(2,1)}, bf16[4,2,64,512]{3,2,1,0:T(8,128)(2,1)}, bf16[4,2,64,352]{3,2,1,0:T(8,128)(2,1)}) custom-call(bf16[384,4096]{1,0:T(8,128)(2,1)} %tokens.1, bf16[1376,384]{1,0:T(8,128)(2,1)} %bitcast.1, bf16[64,512]{1,0:T(8,128)(2,1)} %basis.1, f32[8,1376]{1,0:T(8,128)} %first.3, ...), custom_call_target="tpu_custom_call" | custom-call | flops 2000000000 | bytes 10000000 | tf_op jit(solution)/shard_map/pallas_call | solution.py:400
  90.5 2.5 %shard_map.77 = (f32[8,1376]{1,0:T(8,128)}, f32[8,1376]{1,0:T(8,128)}, bf16[64,11008]{1,0:T(8,128)(2,1)}) custom-call(f32[8,1376]{1,0:T(8,128)} %get-tuple-element.7.own_grad, f32[8,1376]{1,0:T(8,128)} %first.3, f32[8,1376]{1,0:T(8,128)} %second.3, bf16[4,2,64,512]{3,2,1,0:T(8,128)(2,1)} %get-tuple-element.8.blocks_0_, ...), custom_call_target="tpu_custom_call" | custom-call | flops 100000 | bytes 3000000 | tf_op jit(solution)/shard_map/pallas_call | solution.py:418
